TPU v7x, 32 devices: a whole 2x2x4 slice. The times are simulated.
32 devices in a mesh: span: 4 (over z), shard: 8 (over y, x, core).
Axes of the slice: x: 2, y: 2, z: 4, core: 2. Of those that a mesh axis runs over, the one named last changes fastest.
Arguments:
- tokens: bfloat16 [8192, 1152], P(('span', 'shard')), may hold values from -6 to 6
- out_proj: bfloat16 [1152, 1152], replicated, may hold values from -0.1875 to 0.1875
- phi_mean: float32 [1152], replicated, may hold values from -6 to 6
- phi_rotate: bfloat16 [1152, 576], replicated, may hold values from -0.1875 to 0.1875
- destinations: int32 [8192, 1], P(('span', 'shard')), may hold values from 0 to 3; in each aligned block of 256 rows (0 to 255, 256 to 511, ...) at most 96 rows name the same one
- student_hidden: bfloat16 [12288, 1280], P(('span', 'shard')), may hold values from -6 to 6
- adaptor: bfloat16 [1280, 576], replicated, may hold values from -0.15625 to 0.15625
- master: float32 [1280, 576], P('shard'), may hold values from -0.15625 to 0.15625
- moment_one: float32 [1280, 576], P('shard'), may hold values from -4 to 4
- moment_two: float32 [1280, 576], P('shard'), may hold values from 0.01 to 1
Outputs:
- updated_master: float32 [1280, 576], P('shard')
- updated_first: float32 [1280, 576], P('shard')
- updated_second: float32 [1280, 576], P('shard')
Inputs may be any that keep to these rules, and one draw needn't show every extreme that they name: `destinations`: at most 96 of the 256 rows of one device name one span; some span gets exactly 96.
All inputs are finite; a program needn't handle non-finite values.
Results may differ from a plain program's by a relative error of at most 0.00064.
Values may be sent and summed in bfloat16 or wider, within the bound.
A program may use at most 64 MiB of HBM per device.

v0:
```python
import jax
import jax.numpy as jnp
from jax import lax
from jax.sharding import PartitionSpec as P

ADAM_STEP = 1000


beta_first = 0.9
beta_second = 0.999
adam_epsilon = 1e-08
decay_rate = 0.05
learn_rate = 0.001


def route_slots(destinations, span_count, capacity):
    target_span = destinations[:, 0]
    span_ids = jnp.arange(span_count, dtype=jnp.int32)
    one_hot = (target_span[:, None] == span_ids[None, :]).astype(jnp.int32)
    before = jnp.cumsum(one_hot, axis=0) - one_hot
    slot_rank = jnp.sum(before * one_hot, axis=1)
    counts_out = jnp.sum(one_hot, axis=0)
    return (target_span * capacity + slot_rank, counts_out)


def activate(values):
    return jax.nn.gelu(values.astype(jnp.float32), approximate=False).astype(jnp.bfloat16)


def adam_update(gradient, master, moment_one, moment_two):
    first_new = beta_first * moment_one + (1.0 - beta_first) * gradient
    second_new = beta_second * moment_two + (1.0 - beta_second) * gradient * gradient
    bias_first = 1.0 - beta_first**ADAM_STEP
    bias_second = 1.0 - beta_second**ADAM_STEP
    update_dir = (
        first_new / bias_first / (jnp.sqrt(second_new / bias_second) + adam_epsilon)
        + decay_rate * master
    )
    return (master - learn_rate * update_dir, first_new, second_new)


def reduce_and_step(activated, scaled_error, master, moment_one, moment_two):
    contract = (((0,), (0,)), ((), ()))
    partial_sum = lax.psum_scatter(
        lax.dot_general(activated, scaled_error, contract, preferred_element_type=jnp.float32),
        "shard",
        scatter_dimension=0,
        tiled=True,
    )
    gradient = lax.psum(partial_sum, "span")
    return adam_update(gradient, master, moment_one, moment_two)


def body(
    tokens,
    out_proj,
    phi_mean,
    phi_rotate,
    destinations,
    student_hidden,
    adaptor,
    master,
    moment_one,
    moment_two,
):
    span_count = lax.axis_size("span")
    capacity = student_hidden.shape[0] // span_count
    feature_count = adaptor.shape[1]
    projected = (jnp.dot(tokens, out_proj, preferred_element_type=jnp.float32) - phi_mean).astype(
        jnp.bfloat16
    )
    teacher_target = jnp.dot(projected, phi_rotate, preferred_element_type=jnp.float32).astype(
        jnp.bfloat16
    )
    slot_ids, counts_out = route_slots(destinations, span_count, capacity)
    returned = lax.all_to_all(
        student_hidden.reshape(span_count, capacity, student_hidden.shape[1]),
        "span",
        split_axis=0,
        concat_axis=0,
        tiled=True,
    )
    hidden_rows = returned.reshape(span_count * capacity, student_hidden.shape[1])[slot_ids]
    activated = activate(hidden_rows)
    predicted = jnp.dot(activated, adaptor, preferred_element_type=jnp.float32)
    error_value = predicted - teacher_target.astype(jnp.float32)
    scaled_error = (error_value / feature_count).astype(jnp.bfloat16)
    return reduce_and_step(activated, scaled_error, master, moment_one, moment_two)


def solution(mesh):
    in_specs = (
        P(("span", "shard"), None),
        P(),
        P(),
        P(),
        P(("span", "shard"), None),
        P(("span", "shard"), None),
        P(),
        P("shard", None),
        P("shard", None),
        P("shard", None),
    )
    out_specs = (P("shard", None), P("shard", None), P("shard", None))
    return jax.shard_map(body, mesh=mesh, in_specs=in_specs, out_specs=out_specs, check_vma=False)
```

profile of v0, /device:TPU:0, one launch (start us, length us, event | category | flops | bytes accessed | tf_op | source)
XLA Modules:
  0.0 145.5 jit_solution(12610623017864274132)
XLA Ops:
  7.2 0.0 copy-start
  7.2 0.0 copy-start.3
  7.2 0.0 copy-start.5
  7.2 0.0 copy-start.4
  7.2 6.6 %all-to-all-start = ((bf16[4,96,1280]{2,1,0:T(8,128)(2,1)}), bf16[4,96,1280]{2,1,0:T(8,128)(2,1)}, u32[]{:S(2)}, u32[]{:S(2)}) async-start(bf16[4,96,1280]{2,1,0:T(8,128)(2,1)} %bitcast.29), calls=%async_computation | async-start | bytes 1966080 | tf_op jit(solution)/shard_map/all_to_all | solution.py:76
  13.8 0.0 reduce-scatter.2.cloned.1.call-start
  13.8 0.0 copy-done.3
  13.8 1.2 reduce-window.6
  15.0 0.1 slice.10
  15.1 0.1 copy.13
  15.3 0.1 copy.14
  15.4 0.1 add_bitcast_fusion
  15.5 0.0 copy-done
  15.5 3.7 %fusion.34 = f32[256,576]{1,0:T(8,128)} fusion(bf16[1152,576]{0,1:T(8,128)(2,1)} %param.13, bf16[256,1152]{1,0:T(8,128)(2,1)S(1)} %copy-done.4, bf16[1152,1152]{1,0:T(8,128)(2,1)S(1)} %copy-done, f32[1152]{0:T(1024)S(1)} %copy-done.5), kind=kOutput, calls=%fused_computation.41 | convolution fusion | flops 1020100608 | bytes 5165568 | tf_op jit(solution)/shard_map/dot_general | solution.py:72
  19.2 19.0 %all-to-all-done = bf16[4,96,1280]{2,1,0:T(8,128)(2,1)} async-done(((bf16[4,96,1280]{2,1,0:T(8,128)(2,1)}), bf16[4,96,1280]{2,1,0:T(8,128)(2,1)}, u32[]{:S(2)}, u32[]{:S(2)}) %all-to-all-start) | async-done | bytes 983072 | tf_op jit(solution)/shard_map/all_to_all | solution.py:76
  38.2 3.1 %gather_fusion = bf16[256,1280]{1,0:T(8,128)(2,1)S(1)} fusion(bf16[384,1280]{1,0:T(8,128)(2,1)} %bitcast.1, s32[1024]{0:T(1024)S(1)} %pad_clamp_fusion), kind=kCustom, calls=%fused_computation | custom fusion | bytes 1311744 | tf_op jit(solution)/shard_map/gather | solution.py:83
  41.3 9.6 %fusion.35 = f32[1280,576]{1,0:T(8,128)} fusion(f32[256,576]{1,0:T(8,128)} %fusion.34, bf16[1280,576]{0,1:T(8,128)(2,1)} %param.16, bf16[256,1280]{1,0:T(8,128)(2,1)S(1)} %gather_fusion), kind=kOutput, calls=%fused_computation.42 | convolution fusion | flops 798670848 | bytes 5668864 | tf_op jit(solution)/shard_map/dot_general | solution.py:45
  51.0 0.0 reduce-scatter.2.cloned.1.call-update
  51.0 0.0 all-reduce.2.cloned.1.call-start
  51.0 46.1 %reduce-scatter.2.cloned.1.call-done = f32[160,576]{1,0:T(8,128)} async-done(((f32[1280,576]{1,0:T(8,128)}), f32[160,576]{1,0:T(8,128)}) %reduce-scatter.2.cloned.1.call-update) | async-done | bytes 368656 | tf_op jit(solution)/shard_map/reduce_scatter | solution.py:44
  97.1 0.0 all-reduce.2.cloned.1.call-update
  97.2 39.2 %all-reduce.2.cloned.1.call-done = f32[160,576]{1,0:T(8,128)} async-done(((f32[160,576]{1,0:T(8,128)}), f32[160,576]{1,0:T(8,128)}) %all-reduce.2.cloned.1.call-update) | async-done | bytes 368656 | tf_op jit(solution)/shard_map/psum | solution.py:50
  136.4 0.0 copy-done.1
  136.4 2.3 %multiply_subtract_fusion = (f32[160,576]{1,0:T(8,128)}, f32[160,576]{1,0:T(8,128)}, f32[160,576]{1,0:T(8,128)}) fusion(f32[160,576]{1,0:T(8,128)S(1)} %copy-done.1, f32[160,576]{1,0:T(8,128)} %all-reduce.2.cloned.1.call-done, f32[160,576]{1,0:T(8,128)S(1)} %copy-done.2, f32[160,576]{1,0:T(8,128)} %param.18), kind=kLoop, calls=%fused_computation.73 | loop fusion | flops 1290240 | bytes 2580480 | tf_op jit(solution)/shard_map/sub | solution.py:39
  (11 shorter events, 0.1 us)
Async XLA Ops:
  7.2 8.3 %copy-start = (bf16[1152,1152]{1,0:T(8,128)(2,1)S(1)}, bf16[1152,1152]{1,0:T(8,128)(2,1)}, u32[]{:S(2)}) copy-start(bf16[1152,1152]{1,0:T(8,128)(2,1)} %param.11) | copy-start | bytes 7962628
  7.2 6.6 %copy-start.3 = (s32[256,1]{0,1:T(1,128)S(1)}, s32[256,1]{0,1:T(1,128)}, u32[]{:S(2)}) copy-start(s32[256,1]{0,1:T(1,128)} %param.14) | copy-start | bytes 3076
  7.2 8.3 %copy-start.5 = (f32[1152]{0:T(1024)S(1)}, f32[1152]{0:T(1024)}, u32[]{:S(2)}) copy-start(f32[1152]{0:T(1024)} %param.12) | copy-start | bytes 13828
  7.2 8.3 %copy-start.4 = (bf16[256,1152]{1,0:T(8,128)(2,1)S(1)}, bf16[256,1152]{1,0:T(8,128)(2,1)}, u32[]{:S(2)}) copy-start(bf16[256,1152]{1,0:T(8,128)(2,1)} %param.10) | copy-start | bytes 1769476
  7.2 31.0 %all-to-all-start = ((bf16[4,96,1280]{2,1,0:T(8,128)(2,1)}), bf16[4,96,1280]{2,1,0:T(8,128)(2,1)}, u32[]{:S(2)}, u32[]{:S(2)}) async-start(bf16[4,96,1280]{2,1,0:T(8,128)(2,1)} %bitcast.29), calls=%async_computation | async-start | bytes 1966080 | tf_op jit(solution)/shard_map/all_to_all | solution.py:76
  13.8 83.3 %reduce-scatter.2.cloned.1.call-start = ((), (), s32[]{:S(2)}) async-start(), calls=%async_computation.2 | async-start | bytes 3686400 | tf_op jit(solution)/shard_map/reduce_scatter | solution.py:44
  51.0 85.4 %copy-start.1 = (f32[160,576]{1,0:T(8,128)S(1)}, f32[160,576]{1,0:T(8,128)}, u32[]{:S(2)}) copy-start(f32[160,576]{1,0:T(8,128)} %param.17) | copy-start | bytes 1105924
  51.0 85.4 %copy-start.2 = (f32[160,576]{1,0:T(8,128)S(1)}, f32[160,576]{1,0:T(8,128)}, u32[]{:S(2)}) copy-start(f32[160,576]{1,0:T(8,128)} %param.19) | copy-start | bytes 1105924
  51.0 85.4 %all-reduce.2.cloned.1.call-start = ((), (), s32[]{:S(2)}) async-start(), calls=%async_computation.3 | async-start | bytes 819200 | tf_op jit(solution)/shard_map/psum | solution.py:50
Sparse Core Ops, SparseCore 0:
  51.1 45.9 reduce-scatter.1
  99.5 36.8 all-reduce.1
where the time goes:
time: 146 us
  waiting for transfers between devices  104 us (71%)
  between operations  14.1 us (10%)
  matrix products  13.3 us (9%)
  starting transfers between devices  6.64 us (5%)
  other arithmetic  3.7 us (3%)
  local copies, waits for them, and re-layouts  3.41 us (2%)
    reduce_scatter x1, waiting for transfers between devices, reduce_and_step(): lax.psum_scatter(lax.dot_general(activated, scaled_error, contract, prefe...  46.1 us
    psum x1, waiting for transfers between devices, reduce_and_step(): gradient = lax.psum(partial_sum, 'span')  39.2 us
    all_to_all x1, waiting for transfers between devices, body(): lax.all_to_all(student_hidden.reshape(span_count, capacity, student_hidde...  19 us
    dot_general x1, matrix products, reduce_and_step(): lax.dot_general(activated, scaled_error, contract, preferred_element_type...  9.62 us
    all_to_all x1, starting transfers between devices, body(): lax.all_to_all(student_hidden.reshape(span_count, capacity, student_hidde...  6.59 us
    dot_general x1, matrix products, body(): jnp.dot(projected, phi_rotate, preferred_element_type=jnp.float32)  3.71 us
    gather x1, local copies, waits for them, and re-layouts, body(): returned.reshape(span_count * capacity, student_hidden.shape[1])[slot_ids]  3.1 us
  transfers between devices with their start and end apart: 3, of which 3 were waited for; matrix products, arithmetic and copies ran while one was open for 4% of the time, Pallas kernels for 0%

commit v1 on v0

v1 whole, which is shorter than its diff:
```python
import functools

import jax
import jax.numpy as jnp
from jax import lax
from jax.experimental import pallas as pl
from jax.experimental.pallas import tpu as pltpu
from jax.sharding import PartitionSpec as P

ADAM_STEP = 1000


beta_first = 0.9
beta_second = 0.999
adam_epsilon = 1e-08
decay_rate = 0.05
learn_rate = 0.001

EMPTY = 2.0**100
EMPTY_TEST = 2.0**90
MESH = pl.DeviceIdType.MESH


def adam_update(gradient, master, moment_one, moment_two):
    first_new = beta_first * moment_one + (1.0 - beta_first) * gradient
    second_new = beta_second * moment_two + (1.0 - beta_second) * gradient * gradient
    bias_first = 1.0 - beta_first**ADAM_STEP
    bias_second = 1.0 - beta_second**ADAM_STEP
    update_dir = (
        first_new / bias_first / (jnp.sqrt(second_new / bias_second) + adam_epsilon)
        + decay_rate * master
    )
    return (master - learn_rate * update_dir, first_new, second_new)


def route_slots(destinations, span_count, capacity):
    target_span = destinations[:, 0]
    span_ids = jnp.arange(span_count, dtype=jnp.int32)
    one_hot = (target_span[:, None] == span_ids[None, :]).astype(jnp.int32)
    before = jnp.cumsum(one_hot, axis=0) - one_hot
    slot_rank = jnp.sum(before * one_hot, axis=1)
    return target_span * capacity + slot_rank


def general_body(
    tokens,
    out_proj,
    phi_mean,
    phi_rotate,
    destinations,
    student_hidden,
    adaptor,
    master,
    moment_one,
    moment_two,
):
    span_count = lax.axis_size("span")
    slots = student_hidden.shape[0]
    capacity = slots // span_count
    features = adaptor.shape[1]
    projected = (jnp.dot(tokens, out_proj, preferred_element_type=jnp.float32) - phi_mean).astype(
        jnp.bfloat16
    )
    target = jnp.dot(projected, phi_rotate, preferred_element_type=jnp.float32).astype(jnp.bfloat16)
    slot_ids = route_slots(destinations, span_count, capacity)
    placed = jnp.full((slots, features), EMPTY, jnp.bfloat16).at[slot_ids].set(target)
    arrived = lax.all_to_all(
        placed.reshape(span_count, capacity, features), "span", split_axis=0, concat_axis=0, tiled=True
    ).reshape(slots, features)
    activated = jax.nn.gelu(student_hidden.astype(jnp.float32), approximate=False).astype(jnp.bfloat16)
    predicted = jnp.dot(activated, adaptor, preferred_element_type=jnp.float32)
    wanted = arrived.astype(jnp.float32)
    scaled_error = jnp.where(wanted > EMPTY_TEST, 0.0, (predicted - wanted) / features).astype(
        jnp.bfloat16
    )
    contract = (((0,), (0,)), ((), ()))
    partial_sum = lax.psum_scatter(
        lax.dot_general(activated, scaled_error, contract, preferred_element_type=jnp.float32),
        "shard",
        scatter_dimension=0,
        tiled=True,
    )
    return adam_update(lax.psum(partial_sum, "span"), master, moment_one, moment_two)


SPANS = 4
SHARDS = 8


def chunks_of(features):
    first = features // 2 // 128 * 128
    return ((0, first), (first, features))


def dot(a, b):
    return jnp.dot(a, b, preferred_element_type=jnp.float32)


def step_kernel(
    chunks,
    tokens_hbm,
    proj_hbm,
    mean_hbm,
    rotate_hbm,
    dest_hbm,
    hidden_hbm,
    adaptor_hbm,
    master_hbm,
    one_hbm,
    two_hbm,
    out_master,
    out_first,
    out_second,
    tokens,
    proj,
    mean,
    rotate,
    dest,
    hidden,
    adaptor,
    master,
    one,
    two,
    act,
    act_t,
    pred,
    *rest,
):
    per_chunk, (load_sem, a2a_send, a2a_recv, core_sem, s2_sem, s3_sem, z_send, z_recv) = (
        rest[:-8],
        rest[-8:],
    )
    count = len(per_chunk) // len(chunks)
    buf = [per_chunk[c * count : (c + 1) * count] for c in range(len(chunks))]

    span = lax.axis_index("span")
    me = lax.axis_index("shard")
    core = lax.rem(me, 2)
    my_x = lax.rem(me // 2, 2)
    my_y = me // 4
    core_mate = me + 1 - 2 * core
    x_mate = me + 2 - 4 * my_x
    y_mate = me + 4 - 8 * my_y

    slots, width = hidden.shape
    rows = tokens.shape[0]
    features = adaptor.shape[1]
    cap = slots // SPANS
    block = width // SHARDS
    half = block // 2

    pairs = (
        (tokens_hbm, tokens),
        (proj_hbm, proj),
        (mean_hbm, mean),
        (dest_hbm, dest),
        (rotate_hbm, rotate),
        (hidden_hbm, hidden),
        (adaptor_hbm, adaptor),
        (master_hbm, master),
        (one_hbm, one),
        (two_hbm, two),
    )
    loads = [pltpu.make_async_copy(s, d, load_sem.at[i]) for i, (s, d) in enumerate(pairs)]
    for load in loads:
        load.start()

    barrier = pltpu.get_barrier_semaphore()
    for step in range(1, SPANS):
        pl.semaphore_signal(
            barrier, inc=1, device_id=(lax.rem(span + step, SPANS), me), device_id_type=MESH
        )
    for mate in (core_mate, x_mate, y_mate):
        pl.semaphore_signal(barrier, inc=1, device_id=(span, mate), device_id_type=MESH)

    loads[3].wait()
    wanted = dest[...]
    span_ids = lax.broadcasted_iota(jnp.int32, (16, rows), 0)
    one_hot = jnp.where(span_ids == wanted, 1.0, 0.0)
    earlier = jnp.where(
        lax.broadcasted_iota(jnp.int32, (rows, rows), 0)
        < lax.broadcasted_iota(jnp.int32, (rows, rows), 1),
        1.0,
        0.0,
    ).astype(jnp.bfloat16)
    before = dot(one_hot.astype(jnp.bfloat16), earlier)
    rank = jnp.sum(before * one_hot, axis=0, keepdims=True).astype(jnp.int32)
    slot = wanted * cap + rank
    place = jnp.where(lax.broadcasted_iota(jnp.int32, (slots, rows), 0) == slot, 1.0, 0.0)
    empty = (1.0 - jnp.sum(place, axis=1, keepdims=True)) * EMPTY
    place = place.astype(jnp.bfloat16)

    for i in (0, 1, 2):
        loads[i].wait()
    projected = (dot(tokens[...], proj[...]) - mean[...]).astype(jnp.bfloat16)
    loads[4].wait()
    pl.semaphore_wait(barrier, SPANS - 1 + 3)

    a2a = []
    for c, (lo, hi) in enumerate(chunks):
        t_send, t_recv = buf[c][0], buf[c][1]
        target = dot(projected, rotate[:, lo:hi]).astype(jnp.bfloat16)
        t_send[...] = (dot(place, target) + empty).astype(jnp.bfloat16)
        for step in (2, 3, 1):
            other = lax.rem(span + step, SPANS)
            copy = pltpu.make_async_remote_copy(
                src_ref=t_send.at[pl.ds(pl.multiple_of(other * cap, 16), cap)],
                dst_ref=t_recv.at[pl.ds(pl.multiple_of(span * cap, 16), cap)],
                send_sem=a2a_send.at[c, step - 1],
                recv_sem=a2a_recv.at[c, step - 1],
                device_id=(other, me),
                device_id_type=MESH,
            )
            copy.start()
            a2a.append(copy)
        mine = pl.ds(pl.multiple_of(span * cap, 16), cap)
        t_recv[mine, :] = t_send[mine, :]

    loads[5].wait()
    for j in range(0, width, 128):
        x = hidden[:, j : j + 128].astype(jnp.float32)
        a = (0.5 * x * (1.0 + lax.erf(x * (0.5**0.5)))).astype(jnp.bfloat16)
        act[:, j : j + 128] = a
        act_t[j : j + 128, :] = a.T
    loads[6].wait()
    pred[...] = dot(act[...], adaptor[...])

    sends = []

    def send(src, dst, send_sem, recv_sem, device):
        copy = pltpu.make_async_remote_copy(
            src_ref=src,
            dst_ref=dst,
            send_sem=send_sem,
            recv_sem=recv_sem,
            device_id=device,
            device_id_type=MESH,
        )
        copy.start()
        return copy

    core_copies = {}
    s2_copies = {}
    s3_copies = {}

    def gradient_block(index, error):
        start = pl.multiple_of(index * block, 16)
        return dot(act_t[pl.ds(start, block), :], error)

    def form(c):
        lo, hi = chunks[c]
        t_recv, core_out, core_in, total = buf[c][1], buf[c][2], buf[c][3], buf[c][4]
        for copy in a2a[3 * c : 3 * c + 3]:
            copy.wait_recv()
        t = t_recv[...].astype(jnp.float32)
        error = jnp.where(t > EMPTY_TEST, 0.0, (pred[:, lo:hi] - t) * (1.0 / features)).astype(
            jnp.bfloat16
        )
        for j in range(4):
            core_out[j] = gradient_block(2 * j + 1 - core, error).astype(jnp.bfloat16)
        core_copies[c] = send(
            core_out, core_in, core_sem.at[c, 0], core_sem.at[c, 1], (span, core_mate)
        )
        for j in range(4):
            total[j] = gradient_block(2 * j + core, error)

    def first_axis(c):
        core_in, total = buf[c][3], buf[c][4]
        core_copies[c].wait_recv()
        for h in range(2):
            s2_out, s2_in, kept = buf[c][5 + h], buf[c][7 + h], buf[c][9 + h]
            part = pl.ds(h * half, half)
            for j in range(2):
                away = 2 * j + 1 - my_x if h == 0 else 2 * (1 - my_y) + j
                s2_out[j] = (total[away, part, :] + core_in[away, part, :]).astype(jnp.bfloat16)
            s2_copies[c, h] = send(
                s2_out,
                s2_in,
                s2_sem.at[c, h, 0],
                s2_sem.at[c, h, 1],
                (span, x_mate if h == 0 else y_mate),
            )
            for j in range(2):
                here = 2 * j + my_x if h == 0 else 2 * my_y + j
                kept[j] = total[here, part, :] + core_in[here, part, :]

    def second_axis(c):
        for h in range(2):
            s2_in, kept, s3_out, s3_in = buf[c][7 + h], buf[c][9 + h], buf[c][11 + h], buf[c][13 + h]
            s2_copies[c, h].wait_recv()
            bit = my_y if h == 0 else my_x
            s3_out[...] = kept[1 - bit] + s2_in[1 - bit]
            s3_copies[c, h] = send(
                s3_out,
                s3_in,
                s3_sem.at[c, h, 0],
                s3_sem.at[c, h, 1],
                (span, y_mate if h == 0 else x_mate),
            )

    inner = jnp.logical_and(span >= 1, span <= 2)
    outer = jnp.logical_not(inner)
    near = jnp.where(span < 2, 1 - span, 5 - span)

    def z_copy(c, h, kind):
        z_out, z_one, z_two, z_end = buf[c][15 + h], buf[c][17 + h], buf[c][19 + h], buf[c][21 + h]
        src, dst, other = {
            "in": (z_out, z_one, near),
            "across": (z_out, z_two, 3 - span),
            "back": (z_end, z_end, near),
        }[kind]
        slot_of = {"in": 0, "across": 1, "back": 2}[kind]
        return pltpu.make_async_remote_copy(
            src_ref=src,
            dst_ref=dst,
            send_sem=z_send.at[c, h, slot_of],
            recv_sem=z_recv.at[c, h, slot_of],
            device_id=(other, me),
            device_id_type=MESH,
        )

    def chain_start(c):
        for h in range(2):
            s2_in, kept, s3_in = buf[c][7 + h], buf[c][9 + h], buf[c][13 + h]
            z_out, z_one = buf[c][15 + h], buf[c][17 + h]
            s3_copies[c, h].wait_recv()
            bit = my_y if h == 0 else my_x
            own = kept[bit] + s2_in[bit] + s3_in[...]

            @pl.when(outer)
            def _():
                z_out[...] = own
                z_copy(c, h, "in").start()

            @pl.when(inner)
            def _():
                z_copy(c, h, "in").wait_recv()
                z_out[...] = own + z_one[...]
                z_copy(c, h, "across").start()

    def chain_middle(c):
        for h in range(2):
            z_out, z_two, z_end = buf[c][15 + h], buf[c][19 + h], buf[c][21 + h]

            @pl.when(inner)
            def _():
                z_copy(c, h, "across").wait_recv()
                z_end[...] = z_out[...] + z_two[...]
                z_copy(c, h, "back").start()

    def finish(c):
        lo, hi = chunks[c]
        for h in range(2):
            z_end = buf[c][21 + h]

            @pl.when(outer)
            def _():
                z_copy(c, h, "back").wait_recv()

            part = pl.ds(h * half, half)
            new = adam_update(
                z_end[...], master[part, lo:hi], one[part, lo:hi], two[part, lo:hi]
            )
            out_master[part, lo:hi] = new[0]
            out_first[part, lo:hi] = new[1]
            out_second[part, lo:hi] = new[2]

    form(0)
    first_axis(0)
    second_axis(0)
    chain_start(0)
    form(1)
    first_axis(1)
    chain_middle(0)
    second_axis(1)
    for i in (7, 8, 9):
        loads[i].wait()
    chain_start(1)
    finish(0)
    chain_middle(1)
    finish(1)

    for copy in a2a:
        copy.wait_send()
    for c in range(len(chunks)):
        core_copies[c].wait_send()
        for h in range(2):
            s2_copies[c, h].wait_send()
            s3_copies[c, h].wait_send()

            @pl.when(outer)
            def _():
                z_copy(c, h, "in").wait_send()

            @pl.when(inner)
            def _():
                z_copy(c, h, "across").wait_send()
                z_copy(c, h, "back").wait_send()


def kernel_body(
    tokens,
    out_proj,
    phi_mean,
    phi_rotate,
    destinations,
    student_hidden,
    adaptor,
    master,
    moment_one,
    moment_two,
):
    rows = tokens.shape[0]
    slots, width = student_hidden.shape
    features = adaptor.shape[1]
    block = width // SHARDS
    half = block // 2
    chunks = chunks_of(features)
    bf16, f32 = jnp.bfloat16, jnp.float32
    mean = phi_mean.reshape(1, -1)
    dest = destinations.reshape(1, rows)
    inputs = (
        tokens,
        out_proj,
        mean,
        phi_rotate,
        dest,
        student_hidden,
        adaptor,
        master,
        moment_one,
        moment_two,
    )
    scratch = [pltpu.VMEM(a.shape, a.dtype) for a in inputs]
    scratch += [
        pltpu.VMEM((slots, width), bf16),
        pltpu.VMEM((width, slots), bf16),
        pltpu.VMEM((slots, features), f32),
    ]
    for lo, hi in chunks:
        wide = hi - lo
        scratch += [pltpu.VMEM((slots, wide), bf16)] * 2
        scratch += [pltpu.VMEM((4, block, wide), bf16)] * 2
        scratch += [pltpu.VMEM((4, block, wide), f32)]
        scratch += [pltpu.VMEM((2, half, wide), bf16)] * 4
        scratch += [pltpu.VMEM((2, half, wide), f32)] * 2
        scratch += [pltpu.VMEM((half, wide), f32)] * 12
    n = len(chunks)
    dma = pltpu.SemaphoreType.DMA
    scratch += [
        dma((len(inputs),)),
        dma((n, SPANS - 1)),
        dma((n, SPANS - 1)),
        dma((n, 2)),
        dma((n, 2, 2)),
        dma((n, 2, 2)),
        dma((n, 2, 3)),
        dma((n, 2, 3)),
    ]
    flops = 2 * (rows * tokens.shape[1] * (tokens.shape[1] + features) + 2 * slots * width * features)
    return pl.pallas_call(
        functools.partial(step_kernel, chunks),
        out_shape=[jax.ShapeDtypeStruct(master.shape, f32)] * 3,
        in_specs=[pl.BlockSpec(memory_space=pl.ANY)] * len(inputs),
        out_specs=[pl.BlockSpec(memory_space=pltpu.VMEM)] * 3,
        scratch_shapes=scratch,
        compiler_params=pltpu.CompilerParams(
            collective_id=0, has_side_effects=True, vmem_limit_bytes=48 * 2**20
        ),
        cost_estimate=pl.CostEstimate(
            flops=flops, bytes_accessed=10 * 2**20, transcendentals=slots * width
        ),
    )(*inputs)


def solution(mesh):
    in_specs = (
        P(("span", "shard"), None),
        P(),
        P(),
        P(),
        P(("span", "shard"), None),
        P(("span", "shard"), None),
        P(),
        P("shard", None),
        P("shard", None),
        P("shard", None),
    )
    out_specs = (P("shard", None), P("shard", None), P("shard", None))
    tuned = mesh.shape["span"] == SPANS and mesh.shape["shard"] == SHARDS
    body = kernel_body if tuned else general_body
    return jax.shard_map(body, mesh=mesh, in_specs=in_specs, out_specs=out_specs, check_vma=False)
```

time: 146 us -> 63.6 us (0.44)
  waiting for transfers between devices: 104 us -> 0 us
  Pallas kernels: 0 us -> 52.7 us
  between operations: 14.1 us -> 0.7 us
  matrix products: 13.3 us -> 0 us
  starting transfers between devices: 6.64 us -> 0 us
  local copies, waits for them, and re-layouts: 3.41 us -> 9.87 us
  other arithmetic: 3.7 us -> 0 us
    pallas_call x0 -> x1, Pallas kernels: none -> 52.7 us  [kernel_body(): pl.pallas_call(functools.partial(step_kernel, chunks), out_shape=[jax.Sha...]
    reduce_scatter x1 -> x0, waiting for transfers between devices: 46.1 us -> none  [reduce_and_step(): lax.psum_scatter(lax.dot_general(activated, scaled_error, contract, prefe...]
    psum x1 -> x0, waiting for transfers between devices: 39.2 us -> none  [reduce_and_step(): gradient = lax.psum(partial_sum, 'span')]
    all_to_all x1 -> x0, waiting for transfers between devices: 19 us -> none  [body(): lax.all_to_all(student_hidden.reshape(span_count, capacity, student_hidde...]
    dot_general x2 -> x0, matrix products: 13.3 us -> none  [the longest x1 9.62 us: reduce_and_step(): lax.dot_general(activated, scaled_error, contract, preferred_element_type...]
    unnamed x12 -> x17, local copies, waits for them, and re-layouts: 0.03 us -> 9.17 us
    all_to_all x1 -> x0, starting transfers between devices: 6.59 us -> none  [body(): lax.all_to_all(student_hidden.reshape(span_count, capacity, student_hidde...]
    gather x1 -> x0, local copies, waits for them, and re-layouts: 3.1 us -> none  [body(): returned.reshape(span_count * capacity, student_hidden.shape[1])[slot_ids]]
  transfers between devices with their start and end apart: 3 -> 0, of which waited for: 3 -> 0; matrix products, arithmetic and copies ran while one was open for 4% -> 0% of each run, Pallas kernels for 0% -> 0%
where the time goes in v1:
time: 63.6 us; the launch traced here: 63.3 us
  Pallas kernels  52.7 us (83%)
  local copies, waits for them, and re-layouts  9.87 us (16%)
  between operations  0.7 us (1%)
    pallas_call x1, Pallas kernels, kernel_body(): pl.pallas_call(functools.partial(step_kernel, chunks), out_shape=[jax.Sha...  52.7 us
    unnamed x17, local copies, waits for them, and re-layouts  9.17 us

profile of v1, /device:TPU:0, one launch (start us, length us, event | category | flops | bytes accessed | tf_op | source)
XLA Modules:
  0.0 63.3 jit_solution(1693264817007489661)
XLA Ops:
  0.6 0.7 %reshape.12.mean_hbm = f32[1,1152]{1,0:T(1,128)S(1)} reshape(f32[1152]{0:T(1024)} %param.12) | data formatting | bytes 9216 | tf_op jit(solution)/shard_map/reshape | solution.py:420
  1.3 2.1 %copy.13.rotate_hbm = bf16[1152,576]{1,0:T(8,128)(2,1)S(1)} copy(bf16[1152,576]{0,1:T(8,128)(2,1)} %param.13) | data formatting | bytes 2654208 | tf_op args[3]
  3.4 0.0 copy-start
  3.4 0.0 copy-start.1
  3.4 0.0 copy-start.2
  3.5 0.0 copy-start.5
  3.5 2.8 %copy.14.adaptor_hbm = bf16[1280,576]{1,0:T(8,128)(2,1)} copy(bf16[1280,576]{0,1:T(8,128)(2,1)} %param.16) | data formatting | bytes 2949120 | tf_op args[6]
  6.3 0.0 copy-done
  6.3 0.0 copy-done.1
  6.3 0.0 copy-done.2
  6.3 0.0 copy-done.5
  6.3 0.0 copy-start.3
  6.3 1.0 %copy-done.3 = f32[160,576]{1,0:T(8,128)S(1)} copy-done((f32[160,576]{1,0:T(8,128)S(1)}, f32[160,576]{1,0:T(8,128)}, u32[]{:S(2)}) %copy-start.3) | copy-done | bytes 368664
  7.3 0.0 copy-start.4
  7.3 1.0 %copy-done.4 = f32[160,576]{1,0:T(8,128)S(1)} copy-done((f32[160,576]{1,0:T(8,128)S(1)}, f32[160,576]{1,0:T(8,128)}, u32[]{:S(2)}) %copy-start.4) | copy-done | bytes 368664
  8.3 52.7 %shard_map.121 = (f32[160,576]{1,0:T(8,128)S(1)}, f32[160,576]{1,0:T(8,128)S(1)}, f32[160,576]{1,0:T(8,128)S(1)}) custom-call(bf16[256,1152]{1,0:T(8,128)(2,1)S(1)} %copy-done.1, bf16[1152,1152]{1,0:T(8,128)(2,1)} %proj_hbm.1, f32[1,1152]{1,0:T(1,128)S(1)} %reshape.12.mean_hbm, bf16[1152,576]{1,0:T(8,128)(2,1)S(1)} %copy.13.rotate_hbm, ...), custom_call_target="tpu_custom_call" | custom-call | flops 2151677952 | bytes 10485760 | tf_op jit(solution)/shard_map/pallas_call | solution.py:461
  61.1 0.8 %copy.18 = f32[160,576]{1,0:T(8,128)} copy(f32[160,576]{1,0:T(8,128)S(1)} %get-tuple-element.6) | data formatting | bytes 737280
  61.8 0.8 %copy.19 = f32[160,576]{1,0:T(8,128)} copy(f32[160,576]{1,0:T(8,128)S(1)} %get-tuple-element.7) | data formatting | bytes 737280
  62.6 0.8 %copy.20 = f32[160,576]{1,0:T(8,128)} copy(f32[160,576]{1,0:T(8,128)S(1)} %get-tuple-element.8) | data formatting | bytes 737280
Async XLA Ops:
  3.4 2.9 %copy-start = (bf16[384,1280]{1,0:T(8,128)(2,1)S(1)}, bf16[384,1280]{1,0:T(8,128)(2,1)}, u32[]{:S(2)}) copy-start(bf16[384,1280]{1,0:T(8,128)(2,1)} %hidden_hbm.1) | copy-start | bytes 2949124
  3.4 2.9 %copy-start.1 = (bf16[256,1152]{1,0:T(8,128)(2,1)S(1)}, bf16[256,1152]{1,0:T(8,128)(2,1)}, u32[]{:S(2)}) copy-start(bf16[256,1152]{1,0:T(8,128)(2,1)} %tokens_hbm.1) | copy-start | bytes 1769476
  3.4 2.8 %copy-start.2 = (f32[160,576]{1,0:T(8,128)S(1)}, f32[160,576]{1,0:T(8,128)}, u32[]{:S(2)}) copy-start(f32[160,576]{1,0:T(8,128)} %master_hbm.1) | copy-start | bytes 1105924
  3.5 2.8 %copy-start.5 = (s32[256,1]{0,1:T(1,128)S(1)}, s32[256,1]{0,1:T(1,128)}, u32[]{:S(2)}) copy-start(s32[256,1]{0,1:T(1,128)} %param.14) | copy-start | bytes 3076
  6.3 1.0 %copy-start.3 = (f32[160,576]{1,0:T(8,128)S(1)}, f32[160,576]{1,0:T(8,128)}, u32[]{:S(2)}) copy-start(f32[160,576]{1,0:T(8,128)} %one_hbm.1) | copy-start | bytes 1105924
  7.3 1.0 %copy-start.4 = (f32[160,576]{1,0:T(8,128)S(1)}, f32[160,576]{1,0:T(8,128)}, u32[]{:S(2)}) copy-start(f32[160,576]{1,0:T(8,128)} %two_hbm.1) | copy-start | bytes 1105924

commit v2 on v1

--- a/solution.py
+++ b/solution.py
@@ -88,12 +88,17 @@
 
 
 def chunks_of(features):
-    first = features // 2 // 128 * 128
-    return ((0, first), (first, features))
+    last = features // 128 * 128
+    first = last // 256 * 128
+    return ((0, first), (first, last), (last, features))
 
 
 def dot(a, b):
     return jnp.dot(a, b, preferred_element_type=jnp.float32)
+
+
+def dot_t(a, b):
+    return lax.dot_general(a, b, (((1,), (1,)), ((), ())), preferred_element_type=jnp.float32)
 
 
 def step_kernel(
@@ -144,7 +149,7 @@
 
     slots, width = hidden.shape
     rows = tokens.shape[0]
-    features = adaptor.shape[1]
+    features = adaptor.shape[0]
     cap = slots // SPANS
     block = width // SHARDS
     half = block // 2
@@ -192,14 +197,14 @@
 
     for i in (0, 1, 2):
         loads[i].wait()
-    projected = (dot(tokens[...], proj[...]) - mean[...]).astype(jnp.bfloat16)
+    projected = (dot(tokens[...], proj[...]) - mean[...].reshape(1, -1)).astype(jnp.bfloat16)
     loads[4].wait()
     pl.semaphore_wait(barrier, SPANS - 1 + 3)
 
     a2a = []
     for c, (lo, hi) in enumerate(chunks):
         t_send, t_recv = buf[c][0], buf[c][1]
-        target = dot(projected, rotate[:, lo:hi]).astype(jnp.bfloat16)
+        target = dot_t(projected, rotate[lo:hi, :]).astype(jnp.bfloat16)
         t_send[...] = (dot(place, target) + empty).astype(jnp.bfloat16)
         for step in (2, 3, 1):
             other = lax.rem(span + step, SPANS)
@@ -223,7 +228,7 @@
         act[:, j : j + 128] = a
         act_t[j : j + 128, :] = a.T
     loads[6].wait()
-    pred[...] = dot(act[...], adaptor[...])
+    pred[...] = dot_t(act[...], adaptor[...])
 
     sends = []
 
@@ -372,13 +377,19 @@
     form(1)
     first_axis(1)
     chain_middle(0)
+    form(2)
     second_axis(1)
+    first_axis(2)
+    chain_start(1)
+    second_axis(2)
     for i in (7, 8, 9):
         loads[i].wait()
-    chain_start(1)
     finish(0)
     chain_middle(1)
+    chain_start(2)
     finish(1)
+    chain_middle(2)
+    finish(2)
 
     for copy in a2a:
         copy.wait_send()
@@ -417,16 +428,15 @@
     half = block // 2
     chunks = chunks_of(features)
     bf16, f32 = jnp.bfloat16, jnp.float32
-    mean = phi_mean.reshape(1, -1)
     dest = destinations.reshape(1, rows)
     inputs = (
         tokens,
         out_proj,
-        mean,
-        phi_rotate,
+        phi_mean,
+        phi_rotate.T,
         dest,
         student_hidden,
-        adaptor,
+        adaptor.T,
         master,
         moment_one,
         moment_two,
@@ -465,7 +475,7 @@
         out_specs=[pl.BlockSpec(memory_space=pltpu.VMEM)] * 3,
         scratch_shapes=scratch,
         compiler_params=pltpu.CompilerParams(
-            collective_id=0, has_side_effects=True, vmem_limit_bytes=48 * 2**20
+            collective_id=0, has_side_effects=True, vmem_limit_bytes=62 * 2**20
         ),
         cost_estimate=pl.CostEstimate(
             flops=flops, bytes_accessed=10 * 2**20, transcendentals=slots * width

time: 63.6 us -> 55.4 us (0.87)
  local copies, waits for them, and re-layouts: 9.87 us -> 4.36 us
  Pallas kernels: 52.7 us -> 50.2 us
    unnamed x17 -> x5, local copies, waits for them, and re-layouts: 9.17 us -> 4.36 us
    pallas_call x1, Pallas kernels: 52.7 us -> 50.2 us  [kernel_body(): pl.pallas_call(functools.partial(step_kernel, chunks), out_shape=[jax.Sha...]
    reshape x1 -> x0, local copies, waits for them, and re-layouts: 0.7 us -> none  [kernel_body(): mean = phi_mean.reshape(1, -1)]
where the time goes in v2:
time: 55.4 us; the launch traced here: 55.2 us
  Pallas kernels  50.2 us (91%)
  local copies, waits for them, and re-layouts  4.36 us (8%)
  between operations  0.65 us (1%)
    pallas_call x1, Pallas kernels, kernel_body(): pl.pallas_call(functools.partial(step_kernel, chunks), out_shape=[jax.Sha...  50.2 us
    unnamed x5, local copies, waits for them, and re-layouts  4.36 us

profile of v2, /device:TPU:0, one launch (start us, length us, event | category | flops | bytes accessed | tf_op | source)
XLA Modules:
  0.0 55.2 jit_solution(1445687116995969044)
XLA Ops:
  0.6 50.2 %shard_map.121 = (f32[160,576]{1,0:T(8,128)}, f32[160,576]{1,0:T(8,128)}, f32[160,576]{1,0:T(8,128)}) custom-call(bf16[256,1152]{1,0:T(8,128)(2,1)} %tokens_hbm.1, bf16[1152,1152]{1,0:T(8,128)(2,1)} %proj_hbm.1, f32[1152]{0:T(1024)} %mean_hbm.1, bf16[576,1152]{1,0:T(8,128)(2,1)} %bitcast.4, s32[1,256]{1,0:T(1,128)} %bitcast.5, bf16[384,1280]{1,0:T(8,128)(2,1)} %hidden_hbm.1, ...), custom_call_target="tpu_custom_call" | custom-call | flops 2151677952 | bytes 10485760 | tf_op jit(solution)/shard_map/pallas_call | solution.py:471
  50.8 0.0 copy-start
  50.9 1.8 %copy.16 = f32[160,576]{1,0:T(8,128)} copy(f32[160,576]{1,0:T(8,128)} %get-tuple-element.6) | data formatting | bytes 737280
  52.7 1.8 %copy.17 = f32[160,576]{1,0:T(8,128)} copy(f32[160,576]{1,0:T(8,128)} %get-tuple-element.7) | data formatting | bytes 737280
  54.5 0.0 copy-done
  54.5 0.8 %copy.18 = f32[160,576]{1,0:T(8,128)} copy(f32[160,576]{1,0:T(8,128)S(1)} %copy-done) | data formatting | bytes 737280
Async XLA Ops:
  50.8 3.6 %copy-start = (f32[160,576]{1,0:T(8,128)S(1)}, f32[160,576]{1,0:T(8,128)}, u32[]{:S(2)}) copy-start(f32[160,576]{1,0:T(8,128)} %get-tuple-element.8) | copy-start | bytes 1105924
